TPU v7x, 32 devices: a whole 2x2x4 slice. The times are simulated.
32 devices in a mesh: members: 2 (over x), lon: 16 (over z, y, core).
Axes of the slice: x: 2, y: 2, z: 4, core: 2. Of those that a mesh axis runs over, the one named last changes fastest.
Arguments:
- mesh_latent: bfloat16 [8192, 512], P(('members', 'lon')), parts along dimension 0, may hold values from -6 to 6
- grid_latent: bfloat16 [49152, 512], P(('members', 'lon')), parts along dimension 0, may hold values from -6 to 6
- edge_tiles: bfloat16 [192, 8, 128, 128], P('lon'), may hold values from -0.1875 to 0.1875
- sender_ids: int32 [192, 8], P('lon'), may hold values from 0 to 31, as said below
- block_count: int32 [192], P('lon'), may hold values from 1 to 8, as said below
- w_send: bfloat16 [512, 512], replicated, may hold values from -0.25 to 0.25
- w_grid: bfloat16 [512, 512], replicated, may hold values from -0.25 to 0.25
- w_agg: bfloat16 [512, 512], replicated, may hold values from -0.25 to 0.25
- w_out: bfloat16 [83, 512], replicated, may hold values from -0.25 to 0.25
- cotangent: bfloat16 [166, 24576], P('members', 'lon'), parts along dimension 0, may hold values from -6 to 6
Outputs:
- predictions: float32 [166, 24576], P('members', 'lon'), parts along dimension 0
- grad_mesh: float32 [8192, 512], P(('members', 'lon')), parts along dimension 0
- grad_grid: float32 [49152, 512], P(('members', 'lon')), parts along dimension 0
There are 2 independent parts, one for each index of `members`. A program takes and returns all parts, laid end to end along the dimension named above; an argument that names none is the same for every part. Nothing has to cross between parts.
Inputs may be any that keep to these rules, and one draw needn't show every extreme that they name: sender_ids[r, k] names a mesh block of the index of lon that holds receiver block r or of one of its two neighbours on the loop: ((r // 12 + j) * 2 + i) mod 32 with j in -1, 0, 1 and 0 <= i < 2; in slot 0, j is -1 for the first receiver block of each index of lon and +1 for the second. `block_count`: some receiver block uses all 8 slots.
All inputs are finite; a program needn't handle non-finite values.
Results may differ from a plain program's by a relative error of at most 0.0055.
Values may be sent and summed in bfloat16 or wider, within the bound.
A program may use at most 128 MiB of HBM per device.

v0:
```python
import jax
import jax.numpy as jnp
from jax import lax
from jax.sharding import PartitionSpec as P


def shifted(value, axis, steps):
    count = lax.axis_size(axis)
    pairs = [(source, (source + steps) % count) for source in range(count)]
    return lax.ppermute(value, axis, pairs)


def with_halo(array, sides, width):
    for axis, dim in sides:
        count, length = (lax.axis_size(axis), array.shape[dim])
        up = [(i, (i + 1) % count) for i in range(count)]
        down = [(j, i) for i, j in up]
        last = lax.slice_in_dim(array, length - width, length, axis=dim)
        first = lax.slice_in_dim(array, 0, width, axis=dim)
        before = lax.ppermute(last, axis, up)
        after = lax.ppermute(first, axis, down)
        array = jnp.concatenate([before, array, after], axis=dim)
    return array


def silu_grad(value):
    gate = jax.nn.sigmoid(value)
    return gate * (1.0 + value * (1.0 - gate))


def return_rims(lower_part, upper_part):
    from_upper = shifted(lower_part, "lon", -1)
    from_lower = shifted(upper_part, "lon", 1)
    return from_upper + from_lower


def per_device(
    mesh_latent,
    grid_latent,
    edge_tiles,
    sender_ids,
    block_count,
    w_send,
    w_grid,
    w_agg,
    w_out,
    cotangent,
):
    lanes = lax.axis_size("lon")
    place = lax.axis_index("lon")
    recv_blocks, slots, side, _ = edge_tiles.shape
    width = mesh_latent.shape[1]
    rows = mesh_latent.shape[0]
    own_blocks = rows // side
    total_blocks = own_blocks * lanes
    relative = jnp.mod(sender_ids - place * own_blocks + own_blocks, total_blocks)
    live = jnp.arange(slots, dtype=jnp.int32)[None, :] < block_count[:, None]
    live_tiles = jnp.where(live[:, :, None, None], edge_tiles, jnp.zeros((), edge_tiles.dtype))
    mesh_pre = jnp.dot(mesh_latent, w_send, preferred_element_type=jnp.float32)
    sender = jax.nn.silu(mesh_pre).astype(jnp.bfloat16)
    extended = with_halo(sender, (("lon", 0),), rows)
    wide_blocks = extended.reshape(3 * own_blocks, side, width)
    picked = jnp.take(wide_blocks, relative, axis=0)
    aggregated = jnp.einsum(
        "rkab,rkbd->rad", live_tiles, picked, preferred_element_type=jnp.float32
    )
    aggregated = aggregated.astype(jnp.bfloat16).reshape(recv_blocks * side, width)
    pre = jnp.dot(grid_latent, w_grid, preferred_element_type=jnp.float32) + jnp.dot(
        aggregated, w_agg, preferred_element_type=jnp.float32
    )
    hidden = jax.nn.silu(pre).astype(jnp.bfloat16)
    predictions = lax.dot_general(
        w_out, hidden, (((1,), (1,)), ((), ())), preferred_element_type=jnp.float32
    )
    d_hidden = lax.dot_general(
        cotangent, w_out, (((0,), (0,)), ((), ())), preferred_element_type=jnp.float32
    )
    d_pre = (d_hidden * silu_grad(pre)).astype(jnp.bfloat16)
    grad_grid = lax.dot_general(
        d_pre, w_grid, (((1,), (1,)), ((), ())), preferred_element_type=jnp.float32
    )
    d_agg = lax.dot_general(
        d_pre, w_agg, (((1,), (1,)), ((), ())), preferred_element_type=jnp.float32
    ).astype(jnp.bfloat16)
    d_agg = d_agg.reshape(recv_blocks, side, width)
    pieces = jnp.einsum("rkab,rad->rkbd", live_tiles, d_agg, preferred_element_type=jnp.float32)
    empty_wide = jnp.zeros((3 * own_blocks, side, width), jnp.float32)
    d_wide = empty_wide.at[relative.reshape(-1)].add(
        pieces.reshape(recv_blocks * slots, side, width)
    )
    d_wide = d_wide.reshape(3 * rows, width)
    d_sender = d_wide[rows : 2 * rows] + return_rims(d_wide[:rows], d_wide[2 * rows :])
    d_mesh_pre = (d_sender * silu_grad(mesh_pre)).astype(jnp.bfloat16)
    grad_mesh = lax.dot_general(
        d_mesh_pre, w_send, (((1,), (1,)), ((), ())), preferred_element_type=jnp.float32
    )
    return (predictions, grad_mesh, grad_grid)


def solution(mesh):
    placed = (
        P(("members", "lon"), None),
        P(("members", "lon"), None),
        P("lon", None, None, None),
        P("lon", None),
        P("lon"),
        P(),
        P(),
        P(),
        P(),
        P("members", "lon"),
    )
    return jax.shard_map(
        per_device,
        mesh=mesh,
        in_specs=placed,
        out_specs=(P("members", "lon"), P(("members", "lon"), None), P(("members", "lon"), None)),
        check_vma=False,
    )
```

profile of v0, /device:TPU:0, one launch (start us, length us, event | category | flops | bytes accessed | tf_op | source)
XLA Modules:
  0.0 97.1 jit_solution(5593886025112618346)
XLA Ops:
  0.6 0.0 copy-start
  0.6 0.0 copy-start.5
  0.7 2.4 %multiply_convert_fusion.2 = (bf16[256,512]{1,0:T(8,128)(2,1)S(1)}, f32[256,512]{1,0:T(8,128)}) fusion(bf16[256,512]{1,0:T(8,128)(2,1)} %param.10, bf16[512,512]{1,0:T(8,128)(2,1)} %param.15), kind=kOutput, calls=%fused_computation.22 | convolution fusion | flops 134873088 | bytes 1572864 | tf_op jit(solution)/shard_map/dot_general | solution.py:59
  3.0 5.4 %collective-permute-start.1 = (bf16[256,512]{1,0:T(8,128)(2,1)S(1)}, bf16[256,512]{1,0:T(8,128)(2,1)S(1)}, u32[]{:S(2)}, u32[]{:S(2)}) collective-permute-start(bf16[256,512]{1,0:T(8,128)(2,1)S(1)} %get-tuple-element.8), channel_id=1, source_target_pairs={{1,0},{2,1},{3,2},{4,3},{5,4},{6,5},{7,6},{8,7},{9,8},{10,9},{11,1... | collective-permute-start | bytes 786440 | tf_op jit(solution)/shard_map/ppermute | solution.py:21
  8.5 0.0 collective-permute-start
  8.5 0.7 compare_and_fusion
  9.2 0.1 copy.19
  9.3 0.1 copy.18
  9.3 0.1 reshape.86
  9.4 0.1 reshape.81
  9.5 0.0 copy-done
  9.5 0.0 copy-done.5
  9.6 0.0 copy-start.9
  9.6 2.6 %fusion.19 = f32[1536,512]{1,0:T(8,128)} fusion(bf16[1536,512]{1,0:T(8,128)(2,1)S(1)} %copy-done, bf16[512,512]{1,0:T(8,128)(2,1)S(1)} %copy-done.5), kind=kOutput, calls=%fused_computation.39 | convolution fusion | flops 805306368 | bytes 5242880 | tf_op jit(solution)/shard_map/dot_general | solution.py:68
  12.2 0.1 copy.17
  12.3 0.0 copy-done.9
  12.3 0.1 iota_compare_fusion
  12.4 0.0 collective-permute-done.1
  12.4 4.7 %collective-permute-done = bf16[256,512]{1,0:T(8,128)(2,1)} collective-permute-done((bf16[256,512]{1,0:T(8,128)(2,1)S(1)}, bf16[256,512]{1,0:T(8,128)(2,1)}, u32[]{:S(2)}, u32[]{:S(2)}) %collective-permute-start) | collective-permute-done | bytes 262176 | tf_op jit(solution)/shard_map/ppermute | solution.py:20
  17.1 1.0 %pad_maximum_fusion = bf16[768,512]{1,0:T(8,128)(2,1)S(1)} fusion(bf16[256,512]{1,0:T(8,128)(2,1)S(1)} %collective-permute-done.1, bf16[256,512]{1,0:T(8,128)(2,1)S(1)} %get-tuple-element.8, bf16[256,512]{1,0:T(8,128)(2,1)} %collective-permute-done), kind=kLoop, calls=%fused_computation.18 | loop fusion | flops 2359296 | bytes 1572864 | tf_op jit(solution)/shard_map/concatenate | solution.py:22
  18.1 6.8 %gather_fusion = bf16[96,128,512]{2,1,0:T(8,128)(2,1)} fusion(bf16[6,128,512]{2,1,0:T(8,128)(2,1)S(1)} %bitcast.40, s32[1024]{0:T(1024)S(1)} %pad_clamp_fusion), kind=kCustom, calls=%fused_computation | custom fusion | bytes 25166208 | tf_op jit(solution)/shard_map/jit(_take)/gather | solution.py:63
  24.8 0.0 copy-start.1
  24.8 0.0 copy-start.6
  24.8 8.1 %bitcast_convert_fusion = bf16[12,128,512]{2,1,0:T(8,128)(2,1)S(1)} fusion(bf16[12,8,128,512]{3,2,1,0:T(8,128)(2,1)} %bitcast.42, pred[12,8]{1,0:T(8,128)(4,1)S(1)} %copy.17, bf16[12,8,128,128]{3,2,1,0:T(8,128)(2,1)} %param.12, pred[12,8]{1,0:T(8,128)(4,1)S(1)} %iota_compare_fusion), kind=kOutput, calls=%fused_computation.8 | convolution fusion | flops 1619263488 | bytes 17301696 | tf_op jit(solution)/shard_map/rkab,rkbd->rad/dot_general | solution.py:64
  33.0 0.0 copy-done.1
  33.0 0.0 copy-done.6
  33.0 0.0 copy-start.10
  33.0 0.0 copy-start.11
  33.0 1.0 %convolution_add_fusion = f32[1536,512]{1,0:T(8,128)S(1)} fusion(f32[1536,512]{1,0:T(8,128)S(1)} %copy-done.1, bf16[1536,512]{1,0:T(8,128)(2,1)S(1)} %bitcast.44, bf16[512,512]{1,0:T(8,128)(2,1)S(1)} %copy-done.6), kind=kOutput, calls=%fused_computation.7 | convolution fusion | flops 806092800 | bytes 8388608 | tf_op jit(solution)/shard_map/dot_general | solution.py:68
  34.0 0.0 copy-done.10
  34.0 0.0 copy-done.11
  34.1 0.0 copy-start.3
  34.1 1.4 %fusion.4 = bf16[1536,512]{1,0:T(8,128)(2,1)S(1)} fusion(f32[1536,512]{1,0:T(8,128)S(1)} %convolution_add_fusion, bf16[83,1536]{1,0:T(8,128)(2,1)S(1)} %copy-done.10, bf16[83,512]{1,0:T(8,128)(2,1)S(1)} %copy-done.11), kind=kOutput, calls=%fused_computation.13 | convolution fusion | flops 137625600 | bytes 5058560 | tf_op jit(solution)/shard_map/dot_general | solution.py:75
  35.5 0.3 copy-done.3
  35.8 1.0 %convolution_convert_fusion = bf16[1536,512]{1,0:T(8,128)(2,1)S(1)} fusion(bf16[1536,512]{1,0:T(8,128)(2,1)S(1)} %fusion.4, bf16[512,512]{1,0:T(8,128)(2,1)S(1)} %copy-done.6), kind=kOutput, calls=%fused_computation.12 | convolution fusion | flops 806092800 | bytes 3670016 | tf_op jit(solution)/shard_map/dot_general | solution.py:82
  36.8 0.0 copy-start.2
  36.8 2.7 %fusion.21 = f32[1536,512]{1,0:T(8,128)} fusion(bf16[1536,512]{1,0:T(8,128)(2,1)S(1)} %fusion.4, bf16[512,512]{1,0:T(8,128)(2,1)S(1)} %copy-done.5), kind=kOutput, calls=%fused_computation.41 | convolution fusion | flops 805306368 | bytes 5242880 | tf_op jit(solution)/shard_map/dot_general | solution.py:79
  39.6 0.0 copy-done.2
  39.6 10.1 %fusion.5 = f32[12,8,128,512]{3,2,1,0:T(8,128)} fusion(bf16[12,128,512,1]{2,1,3,0:T(8,128)(2,1)S(1)} %bitcast.43, bf16[12,8,128,128]{3,2,1,0:T(8,128)(2,1)S(1)} %copy-done.2, pred[12,8]{1,0:T(8,128)(4,1)S(1)} %iota_compare_fusion), kind=kOutput, calls=%fused_computation.14 | convolution fusion | flops 1612185600 | bytes 29884512 | tf_op jit(solution)/shard_map/rkab,rad->rkbd/dot_general | solution.py:86
  49.7 0.2 broadcast_in_dim.36
  49.9 34.1 %scatter_fusion = f32[6,128,512]{2,1,0:T(8,128)S(1)} fusion(f32[6,128,512]{2,1,0:T(8,128)S(1)} %broadcast_in_dim.36, s32[96]{0:T(128)S(1)} %fusion.13, f32[96,128,512]{2,1,0:T(8,128)} %bitcast.41), kind=kCustom, calls=%fused_computation.1 | custom fusion | flops 6291456 | bytes 75497856 | tf_op jit(solution)/shard_map/scatter-add | solution.py:88
  84.0 0.0 copy-start.4
  84.0 0.2 fusion.18
  84.2 0.1 collective-permute-start.2
  84.3 0.0 copy-start.8
  84.3 0.0 copy-start.7
  84.3 0.5 collective-permute-start.3
  84.8 1.1 %copy-done.4 = f32[1536,512]{1,0:T(8,128)S(1)} copy-done((f32[1536,512]{1,0:T(8,128)S(1)}, f32[1536,512]{1,0:T(8,128)}, u32[]{:S(2)}) %copy-start.4) | copy-done | bytes 3145752
  85.9 1.8 %convolution_bitcast_fusion = f32[83,1536]{1,0:T(8,128)} fusion(bf16[83,512]{1,0:T(8,128)(2,1)S(1)} %copy-done.11, f32[1536,512]{1,0:T(8,128)S(1)} %copy-done.4), kind=kOutput, calls=%fused_computation.15 | convolution fusion | flops 134479872 | bytes 3740672 | tf_op jit(solution)/shard_map/dot_general | solution.py:72
  87.7 3.3 %collective-permute-done.2 = f32[256,512]{1,0:T(8,128)S(1)} collective-permute-done((f32[256,512]{1,0:T(8,128)S(1)}, f32[256,512]{1,0:T(8,128)S(1)}, u32[]{:S(2)}, u32[]{:S(2)}) %collective-permute-start.2) | collective-permute-done | bytes 524320 | tf_op jit(solution)/shard_map/ppermute | solution.py:10
  91.0 4.7 %collective-permute-done.3 = f32[256,512]{1,0:T(8,128)S(1)} collective-permute-done((f32[256,512]{1,0:T(8,128)S(1)}, f32[256,512]{1,0:T(8,128)S(1)}, u32[]{:S(2)}, u32[]{:S(2)}) %collective-permute-start.3) | collective-permute-done | bytes 524320 | tf_op jit(solution)/shard_map/ppermute | solution.py:10
  95.7 0.0 copy-done.8
  95.7 0.3 fusion.11
  96.0 0.0 copy-done.7
  96.0 1.1 %fusion.20 = f32[256,512]{1,0:T(8,128)} fusion(bf16[256,512]{1,0:T(8,128)(2,1)S(1)} %fusion.11, bf16[512,512]{1,0:T(8,128)(2,1)S(1)} %copy-done.7), kind=kOutput, calls=%fused_computation.40 | convolution fusion | flops 134217728 | bytes 1310720 | tf_op jit(solution)/shard_map/dot_general | solution.py:94
  (3 shorter events, 0.0 us)
Async XLA Ops:
  0.6 8.9 %copy-start = (bf16[1536,512]{1,0:T(8,128)(2,1)S(1)}, bf16[1536,512]{1,0:T(8,128)(2,1)}, u32[]{:S(2)}) copy-start(bf16[1536,512]{1,0:T(8,128)(2,1)} %param.11) | copy-start | bytes 4718596
  0.6 8.9 %copy-start.5 = (bf16[512,512]{1,0:T(8,128)(2,1)S(1)}, bf16[512,512]{1,0:T(8,128)(2,1)}, u32[]{:S(2)}) copy-start(bf16[512,512]{1,0:T(8,128)(2,1)} %param.16) | copy-start | bytes 1572868
  3.0 9.4 %collective-permute-start.1 = (bf16[256,512]{1,0:T(8,128)(2,1)S(1)}, bf16[256,512]{1,0:T(8,128)(2,1)S(1)}, u32[]{:S(2)}, u32[]{:S(2)}) collective-permute-start(bf16[256,512]{1,0:T(8,128)(2,1)S(1)} %get-tuple-element.8), channel_id=1, source_target_pairs={{1,0},{2,1},{3,2},{4,3},{5,4},{6,5},{7,6},{8,7},{9,8},{10,9},{11,1... | collective-permute-start | bytes 786440 | tf_op jit(solution)/shard_map/ppermute | solution.py:21
  8.5 8.6 %collective-permute-start = (bf16[256,512]{1,0:T(8,128)(2,1)S(1)}, bf16[256,512]{1,0:T(8,128)(2,1)}, u32[]{:S(2)}, u32[]{:S(2)}) collective-permute-start(bf16[256,512]{1,0:T(8,128)(2,1)S(1)} %get-tuple-element.8), channel_id=1, source_target_pairs={{0,1},{1,2},{2,3},{3,4},{4,5},{5,6},{6,7},{7,8},{8,9},{9,10},{10,1... | collective-permute-start | bytes 786440 | tf_op jit(solution)/shard_map/ppermute | solution.py:20
  9.6 2.8 %copy-start.9 = (s32[12]{0:T(128)S(1)}, s32[12]{0:T(128)}, u32[]{:S(2)}) copy-start(s32[12]{0:T(128)} %param.14) | copy-start | bytes 148
  24.8 8.2 %copy-start.1 = (f32[1536,512]{1,0:T(8,128)S(1)}, f32[1536,512]{1,0:T(8,128)}, u32[]{:S(2)}) copy-start(f32[1536,512]{1,0:T(8,128)} %fusion.19) | copy-start | bytes 9437188
  24.8 8.2 %copy-start.6 = (bf16[512,512]{1,0:T(8,128)(2,1)S(1)}, bf16[512,512]{1,0:T(8,128)(2,1)}, u32[]{:S(2)}) copy-start(bf16[512,512]{1,0:T(8,128)(2,1)} %param.17) | copy-start | bytes 1572868
  33.0 1.0 %copy-start.10 = (bf16[83,1536]{1,0:T(8,128)(2,1)S(1)}, bf16[83,1536]{1,0:T(8,128)(2,1)}, u32[]{:S(2)}) copy-start(bf16[83,1536]{1,0:T(8,128)(2,1)} %param.19) | copy-start | bytes 764932
  33.0 1.0 %copy-start.11 = (bf16[83,512]{1,0:T(8,128)(2,1)S(1)}, bf16[83,512]{1,0:T(8,128)(2,1)}, u32[]{:S(2)}) copy-start(bf16[83,512]{1,0:T(8,128)(2,1)} %param.18) | copy-start | bytes 254980
  34.1 1.7 %copy-start.3 = (f32[1536,512]{1,0:T(8,128)}, f32[1536,512]{1,0:T(8,128)S(1)}, u32[]{:S(2)}) copy-start(f32[1536,512]{1,0:T(8,128)S(1)} %convolution_add_fusion) | copy-start | bytes 9437188
  36.8 2.7 %copy-start.2 = (bf16[12,8,128,128]{3,2,1,0:T(8,128)(2,1)S(1)}, bf16[12,8,128,128]{3,2,1,0:T(8,128)(2,1)}, u32[]{:S(2)}) copy-start(bf16[12,8,128,128]{3,2,1,0:T(8,128)(2,1)} %param.12) | copy-start | bytes 9437188
  84.0 1.9 %copy-start.4 = (f32[1536,512]{1,0:T(8,128)S(1)}, f32[1536,512]{1,0:T(8,128)}, u32[]{:S(2)}) copy-start(f32[1536,512]{1,0:T(8,128)} %copy-done.3) | copy-start | bytes 9437188
  84.2 6.8 %collective-permute-start.2 = (f32[256,512]{1,0:T(8,128)S(1)}, f32[256,512]{1,0:T(8,128)S(1)}, u32[]{:S(2)}, u32[]{:S(2)}) collective-permute-start(f32[256,512]{1,0:T(8,128)S(1)} %bitcast.46), channel_id=1, source_target_pairs={{0,15},{1,0},{2,1},{3,2},{4,3},{5,4},{6,5},{7,6},{8,7},{9,8},{10,9... | collective-permute-start | bytes 1572872 | tf_op jit(solution)/shard_map/ppermute | solution.py:10
  84.3 11.4 %copy-start.8 = (f32[256,512]{1,0:T(8,128)S(1)}, f32[256,512]{1,0:T(8,128)}, u32[]{:S(2)}) copy-start(f32[256,512]{1,0:T(8,128)} %get-tuple-element.9) | copy-start | bytes 1572868
  84.3 11.7 %copy-start.7 = (bf16[512,512]{1,0:T(8,128)(2,1)S(1)}, bf16[512,512]{1,0:T(8,128)(2,1)}, u32[]{:S(2)}) copy-start(bf16[512,512]{1,0:T(8,128)(2,1)} %param.15) | copy-start | bytes 1572868
  84.3 11.4 %collective-permute-start.3 = (f32[256,512]{1,0:T(8,128)S(1)}, f32[256,512]{1,0:T(8,128)S(1)}, u32[]{:S(2)}, u32[]{:S(2)}) collective-permute-start(f32[256,512]{1,0:T(8,128)S(1)} %bitcast.45), channel_id=1, source_target_pairs={{0,1},{1,2},{2,3},{3,4},{4,5},{5,6},{6,7},{7,8},{8,9},{9,10},{10,1... | collective-permute-start | bytes 1572872 | tf_op jit(solution)/shard_map/ppermute | solution.py:10
where the time goes:
time: 97.7 us; the launch traced here: 97.1 us
  other arithmetic  36.2 us (37%)
  matrix products  32.4 us (33%)
  waiting for transfers between devices  12.6 us (13%)
  local copies, waits for them, and re-layouts  9.04 us (9%)
  starting transfers between devices  5.98 us (6%)
    scatter-add x1, other arithmetic, per_device(): empty_wide.at[relative.reshape(-1)]  34.1 us
    dot_general x1, matrix products, per_device(): jnp.einsum('rkab,rad->rkbd', live_tiles, d_agg, preferred_element_type=jn...  10.1 us
    dot_general x1, matrix products, per_device(): jnp.einsum('rkab,rkbd->rad', live_tiles, picked, preferred_element_type=j...  8.14 us
    ppermute x2, waiting for transfers between devices, shifted(): return lax.ppermute(value, axis, pairs)  7.94 us
    gather x1, local copies, waits for them, and re-layouts, per_device(): picked = jnp.take(wide_blocks, relative, axis=0)  6.75 us
    ppermute x1, starting transfers between devices, with_halo(): after = lax.ppermute(first, axis, down)  5.44 us
    ppermute x1, waiting for transfers between devices, with_halo(): before = lax.ppermute(last, axis, up)  4.68 us
    dot_general x1, matrix products, per_device(): lax.dot_general(d_pre, w_grid, (((1,), (1,)), ((), ())), preferred_elemen...  2.72 us
  transfers between devices with their start and end apart: 4, of which 3 were waited for; matrix products, arithmetic and copies ran while one was open for 6% of the time, Pallas kernels for 0%

commit v1 on v0

v1 whole, which is shorter than its diff:
```python
import functools

import jax
import jax.numpy as jnp
from jax import lax
from jax.experimental import pallas as pl
from jax.experimental.pallas import tpu as pltpu
from jax.sharding import PartitionSpec as P

MESH = pl.DeviceIdType.MESH
F32 = jnp.float32
BF16 = jnp.bfloat16


def gate_of(value):
    return 0.5 * jnp.tanh(0.5 * value) + 0.5


def matmul(a, b):
    return jnp.dot(a, b, preferred_element_type=F32)


def kernel(
    lanes,
    ids_ref,
    count_ref,
    mesh_hbm,
    grid_hbm,
    tiles_hbm,
    w_send_hbm,
    w_grid_hbm,
    w_agg_hbm,
    w_out_hbm,
    cot_hbm,
    pred_hbm,
    gmesh_hbm,
    ggrid_hbm,
    mesh_v,
    grid_v,
    tiles_v,
    w_send_v,
    w_grid_v,
    w_agg_v,
    w_out_v,
    cot_v,
    w_send_t,
    w_grid_t,
    w_agg_t,
    mesh_pre_v,
    wide_v,
    dense_v,
    dense_t,
    part_v,
    pre_v,
    dhid_v,
    hidden_v,
    dpre_v,
    dagg_v,
    own_v,
    tx_v,
    rx_v,
    pred_v,
    gmesh_v,
    ggrid_v,
    in_sem,
    grid_sem,
    tile_sem,
    out_sem,
    gout_sem,
    fsend_sem,
    frecv_sem,
    bsend_sem,
    brecv_sem,
):
    me = lax.axis_index("lon")
    right, left = lax.rem(me + 1, lanes), lax.rem(me + lanes - 1, lanes)
    rows = mesh_v.shape[0]
    recv, slots, side, _ = tiles_v.shape
    grid_rows = grid_v.shape[0]
    own = rows // side
    total = own * lanes
    chunk = 2 * side
    chunks = grid_rows // chunk
    big = 4 * side
    bigs = grid_rows // big

    barrier = pltpu.get_barrier_semaphore()
    for neighbour in (left, right):
        pl.semaphore_signal(barrier, inc=1, device_id={"lon": neighbour}, device_id_type=MESH)

    def load(at, src, dst):
        return pltpu.make_async_copy(src, dst, in_sem.at[at])

    loads = [
        load(0, mesh_hbm, mesh_v),
        load(1, w_send_hbm, w_send_v),
        load(2, w_grid_hbm, w_grid_v),
        load(3, w_agg_hbm, w_agg_v),
        load(4, w_out_hbm, w_out_v),
        load(5, cot_hbm, cot_v),
    ]

    def grid_copy(c):
        at = pl.ds(c * chunk, chunk)
        return pltpu.make_async_copy(grid_hbm.at[at], grid_v.at[at], grid_sem.at[c])

    def tile_copy(c):
        at = pl.ds(c * 2, 2)
        return pltpu.make_async_copy(tiles_hbm.at[at], tiles_v.at[at], tile_sem.at[c])

    for c in loads:
        c.start()
    for c in range(chunks):
        grid_copy(c).start()
        tile_copy(c).start()

    loads[0].wait()
    loads[1].wait()
    mesh_pre = matmul(mesh_v[...], w_send_v[...])
    mesh_pre_v[...] = mesh_pre
    wide_v[pl.ds(rows, rows), :] = (mesh_pre * gate_of(mesh_pre)).astype(BF16)

    pl.semaphore_wait(barrier, 2)

    def halo(way):
        target, dst = (right, 0) if way == 0 else (left, 2 * rows)
        return pltpu.make_async_remote_copy(
            src_ref=wide_v.at[pl.ds(rows, rows)],
            dst_ref=wide_v.at[pl.ds(dst, rows)],
            send_sem=fsend_sem.at[way],
            recv_sem=frecv_sem.at[way],
            device_id={"lon": target},
            device_id_type=MESH,
        )

    halos = [halo(0), halo(1)]
    for copy in halos:
        copy.start()

    w_send_t[...] = w_send_v[...].T
    for c in loads[2:]:
        c.wait()
    w_grid_t[...] = w_grid_v[...].T
    w_agg_t[...] = w_agg_v[...].T

    sub = 32

    def early(c, carry):
        grid_copy(c).wait()
        tile_copy(c).wait()
        at = pl.ds(pl.multiple_of(c * chunk, chunk), chunk)
        for q in range(2):
            r = c * 2 + q
            rel = []
            for k in range(slots):
                raw = lax.rem(ids_ref[r, k] - me * own + own + total, total)
                rel.append(jnp.where(k < count_ref[r], raw, -1))
            row0 = pl.multiple_of(r * side, side)
            for s in range(side // sub):
                sums = [None] * (3 * own)
                for k in range(slots):
                    tile = tiles_v[r, k, pl.ds(s * sub, sub), :].astype(F32)
                    for j in range(3 * own):
                        term = tile * jnp.where(rel[k] == j, 1.0, 0.0).astype(F32)
                        sums[j] = term if sums[j] is None else sums[j] + term
                for j in range(3 * own):
                    dense_v[pl.ds(row0 + s * sub, sub), j * side : (j + 1) * side] = sums[
                        j
                    ].astype(BF16)
            for j in range(3 * own):
                block = dense_v[pl.ds(row0, side), j * side : (j + 1) * side]
                dense_t[j * side : (j + 1) * side, pl.ds(row0, side)] = block.T
        pre_v[at, :] = matmul(grid_v[at, :], w_grid_v[...])
        dhid_v[at, :] = lax.dot_general(
            cot_v[:, at], w_out_v[...], (((0,), (0,)), ((), ())), preferred_element_type=F32
        )
        part_v[at, :] = matmul(dense_v[at, rows : 2 * rows], wide_v[rows : 2 * rows, :])
        return carry

    lax.fori_loop(0, chunks, early, 0)

    for copy in halos:
        copy.wait_recv()

    def middle(c, carry):
        at = pl.ds(pl.multiple_of(c * big, big), big)
        agg = part_v[at, :] + matmul(dense_v[at, :rows], wide_v[:rows, :])
        agg = agg + matmul(dense_v[at, 2 * rows :], wide_v[2 * rows :, :])
        pre = pre_v[at, :] + matmul(agg.astype(BF16), w_agg_v[...])
        gate = gate_of(pre)
        hidden_v[at, :] = (pre * gate).astype(BF16)
        d_pre = (dhid_v[at, :] * (gate * (1.0 + pre * (1.0 - gate)))).astype(BF16)
        dpre_v[at, :] = d_pre
        dagg_v[at, :] = matmul(d_pre, w_agg_t[...]).astype(BF16)
        return carry

    lax.fori_loop(0, bigs, middle, 0)

    def rim(way):
        target = left if way == 0 else right
        return pltpu.make_async_remote_copy(
            src_ref=tx_v.at[way],
            dst_ref=rx_v.at[way],
            send_sem=bsend_sem.at[way],
            recv_sem=brecv_sem.at[way],
            device_id={"lon": target},
            device_id_type=MESH,
        )

    rims = [rim(0), rim(1)]
    for way, start in ((0, 0), (1, 2 * rows)):
        tx_v[way] = matmul(dense_t[start : start + rows, :], dagg_v[...]).astype(BF16)
        rims[way].start()
    own_v[...] = matmul(dense_t[rows : 2 * rows, :], dagg_v[...])

    def ggrid_copy(c):
        at = pl.ds(c * big, big)
        return pltpu.make_async_copy(ggrid_v.at[at], ggrid_hbm.at[at], gout_sem.at[c])

    def late(c, carry):
        at = pl.ds(pl.multiple_of(c * big, big), big)
        ggrid_v[at, :] = matmul(dpre_v[at, :], w_grid_t[...])
        ggrid_copy(c).start()
        pred_v[:, at] = lax.dot_general(
            w_out_v[...], hidden_v[at, :], (((1,), (1,)), ((), ())), preferred_element_type=F32
        )
        return carry

    lax.fori_loop(0, bigs, late, 0)
    pred_copy = pltpu.make_async_copy(pred_v, pred_hbm, out_sem.at[0])
    pred_copy.start()

    mesh_pre = mesh_pre_v[...]
    gate = gate_of(mesh_pre)
    slope = gate * (1.0 + mesh_pre * (1.0 - gate))
    for copy in rims:
        copy.wait_recv()
    d_sender = own_v[...] + (rx_v[0].astype(F32) + rx_v[1].astype(F32))
    gmesh_v[...] = matmul((d_sender * slope).astype(BF16), w_send_t[...])
    gmesh_copy = pltpu.make_async_copy(gmesh_v, gmesh_hbm, out_sem.at[1])
    gmesh_copy.start()

    for copy in halos + rims:
        copy.wait_send()
    for c in range(bigs):
        ggrid_copy(c).wait()
    pred_copy.wait()
    gmesh_copy.wait()


def per_device(
    mesh_latent,
    grid_latent,
    edge_tiles,
    sender_ids,
    block_count,
    w_send,
    w_grid,
    w_agg,
    w_out,
    cotangent,
):
    lanes = lax.axis_size("lon")
    rows, width = mesh_latent.shape
    grid_rows = grid_latent.shape[0]
    recv, _, side, _ = edge_tiles.shape
    variables = w_out.shape[0]
    wide = 3 * rows
    anywhere = pl.BlockSpec(memory_space=pl.ANY)
    scalars = pl.BlockSpec(memory_space=pltpu.SMEM)
    chunks = recv // 2
    bigs = recv // 4

    def vmem(*shape, dtype=BF16):
        return pltpu.VMEM(shape, dtype)

    square = (width, width)
    return pl.pallas_call(
        functools.partial(kernel, lanes),
        out_shape=(
            jax.ShapeDtypeStruct((variables, grid_rows), F32),
            jax.ShapeDtypeStruct((rows, width), F32),
            jax.ShapeDtypeStruct((grid_rows, width), F32),
        ),
        in_specs=[scalars] * 2 + [anywhere] * 8,
        out_specs=(anywhere,) * 3,
        scratch_shapes=[
            vmem(rows, width),
            vmem(grid_rows, width),
            vmem(*edge_tiles.shape),
            vmem(*square),
            vmem(*square),
            vmem(*square),
            vmem(variables, width),
            vmem(variables, grid_rows),
            vmem(*square),
            vmem(*square),
            vmem(*square),
            vmem(rows, width, dtype=F32),
            vmem(wide, width),
            vmem(grid_rows, wide),
            vmem(wide, grid_rows),
            vmem(grid_rows, width, dtype=F32),
            vmem(grid_rows, width, dtype=F32),
            vmem(grid_rows, width, dtype=F32),
            vmem(grid_rows, width),
            vmem(grid_rows, width),
            vmem(grid_rows, width),
            vmem(rows, width, dtype=F32),
            vmem(2, rows, width),
            vmem(2, rows, width),
            vmem(variables, grid_rows, dtype=F32),
            vmem(rows, width, dtype=F32),
            vmem(grid_rows, width, dtype=F32),
            pltpu.SemaphoreType.DMA((6,)),
            pltpu.SemaphoreType.DMA((chunks,)),
            pltpu.SemaphoreType.DMA((chunks,)),
            pltpu.SemaphoreType.DMA((2,)),
            pltpu.SemaphoreType.DMA((bigs,)),
            pltpu.SemaphoreType.DMA((2,)),
            pltpu.SemaphoreType.DMA((2,)),
            pltpu.SemaphoreType.DMA((2,)),
            pltpu.SemaphoreType.DMA((2,)),
        ],
        compiler_params=pltpu.CompilerParams(
            collective_id=0, has_side_effects=True, vmem_limit_bytes=56 * 2**20
        ),
        cost_estimate=pl.CostEstimate(
            flops=7_000_000_000, bytes_accessed=11_000_000, transcendentals=1_000_000
        ),
    )(
        sender_ids,
        block_count,
        mesh_latent,
        grid_latent,
        edge_tiles,
        w_send,
        w_grid,
        w_agg,
        w_out,
        cotangent,
    )


def solution(mesh):
    placed = (
        P(("members", "lon"), None),
        P(("members", "lon"), None),
        P("lon", None, None, None),
        P("lon", None),
        P("lon"),
        P(),
        P(),
        P(),
        P(),
        P("members", "lon"),
    )
    return jax.shard_map(
        per_device,
        mesh=mesh,
        in_specs=placed,
        out_specs=(P("members", "lon"), P(("members", "lon"), None), P(("members", "lon"), None)),
        check_vma=False,
    )
```

time: 97.7 us -> 35.4 us (0.36)
  other arithmetic: 36.2 us -> 0 us
  matrix products: 32.4 us -> 0 us
  Pallas kernels: 0 us -> 25.4 us
  waiting for transfers between devices: 12.6 us -> 0 us
  starting transfers between devices: 5.98 us -> 0 us
    scatter-add x1 -> x0, other arithmetic: 34.1 us -> none  [per_device(): empty_wide.at[relative.reshape(-1)]]
    dot_general x10 -> x0, matrix products: 32.4 us -> none  [the longest x1 10.1 us: per_device(): jnp.einsum('rkab,rad->rkbd', live_tiles, d_agg, preferred_element_type=jn...]
    pallas_call x0 -> x1, Pallas kernels: none -> 25.4 us  [per_device(): pl.pallas_call(functools.partial(kernel, lanes), out_shape=(jax.ShapeDtyp...]
    ppermute x4 -> x0, waiting for transfers between devices: 12.6 us -> none  [the longest x2 7.94 us: shifted(): return lax.ppermute(value, axis, pairs)]
    unnamed x24 -> x4, local copies, waits for them, and re-layouts: 1.48 us -> 8.97 us
    gather x1 -> x0, local copies, waits for them, and re-layouts: 6.75 us -> none  [per_device(): picked = jnp.take(wide_blocks, relative, axis=0)]
    ppermute x4 -> x0, starting transfers between devices: 5.98 us -> none  [the longest x1 5.44 us: with_halo(): after = lax.ppermute(first, axis, down)]
    concatenate x1 -> x0, other arithmetic: 1 us -> none  [with_halo(): array = jnp.concatenate([before, array, after], axis=dim)]
  transfers between devices with their start and end apart: 4 -> 0, of which waited for: 3 -> 0; matrix products, arithmetic and copies ran while one was open for 6% -> 0% of each run, Pallas kernels for 0% -> 0%
where the time goes in v1:
time: 35.4 us; the launch traced here: 35 us
  Pallas kernels  25.4 us (72%)
  local copies, waits for them, and re-layouts  8.97 us (25%)
  between operations  0.64 us (2%)
    pallas_call x1, Pallas kernels, per_device(): pl.pallas_call(functools.partial(kernel, lanes), out_shape=(jax.ShapeDtyp...  25.4 us
    unnamed x4, local copies, waits for them, and re-layouts  8.97 us

profile of v1, /device:TPU:0, one launch (start us, length us, event | category | flops | bytes accessed | tf_op | source)
XLA Modules:
  0.0 35.0 jit_solution(9686176982061971219)
XLA Ops:
  0.6 1.4 %copy.13.ids_ref = s32[12,8]{1,0:T(8,128)} copy(s32[12,8]{0,1:T(8,128)} %param.13) | data formatting | bytes 768 | tf_op args[3]
  2.0 25.4 %shard_map.121 = (f32[83,1536]{1,0:T(8,128)}, f32[256,512]{1,0:T(8,128)}, f32[1536,512]{1,0:T(8,128)}) custom-call(s32[12,8]{1,0:T(8,128)} %copy.13.ids_ref, s32[12]{0:T(128)} %count_ref.1, bf16[256,512]{1,0:T(8,128)(2,1)} %mesh_hbm.1, bf16[1536,512]{1,0:T(8,128)(2,1)} %grid_hbm.1, bf16[12,8,128,128]{3,2,1,0:T(8,128)(2,1)} %tiles_hbm.1, ...), custom_call_target="tpu_custom_call" | custom-call | flops 7000000000 | bytes 11000000 | tf_op jit(solution)/shard_map/pallas_call | solution.py:278
  27.4 1.9 %copy.17 = f32[83,1536]{1,0:T(8,128)} copy(f32[83,1536]{1,0:T(8,128)} %get-tuple-element.6) | data formatting | bytes 1019904
  29.3 1.9 %copy.18 = f32[256,512]{1,0:T(8,128)} copy(f32[256,512]{1,0:T(8,128)} %get-tuple-element.7) | data formatting | bytes 1048576
  31.2 3.9 %copy.19 = f32[1536,512]{1,0:T(8,128)} copy(f32[1536,512]{1,0:T(8,128)} %get-tuple-element.8) | data formatting | bytes 6291456

commit v2 on v1

--- a/solution.py
+++ b/solution.py
@@ -33,8 +33,8 @@
     w_out_hbm,
     cot_hbm,
     pred_hbm,
-    gmesh_hbm,
-    ggrid_hbm,
+    dmesh_hbm,
+    dpre_hbm,
     mesh_v,
     grid_v,
     tiles_v,
@@ -43,8 +43,6 @@
     w_agg_v,
     w_out_v,
     cot_v,
-    w_send_t,
-    w_grid_t,
     w_agg_t,
     mesh_pre_v,
     wide_v,
@@ -60,8 +58,7 @@
     tx_v,
     rx_v,
     pred_v,
-    gmesh_v,
-    ggrid_v,
+    dmesh_v,
     in_sem,
     grid_sem,
     tile_sem,
@@ -137,10 +134,8 @@
     for copy in halos:
         copy.start()
 
-    w_send_t[...] = w_send_v[...].T
     for c in loads[2:]:
         c.wait()
-    w_grid_t[...] = w_grid_v[...].T
     w_agg_t[...] = w_agg_v[...].T
 
     sub = 32
@@ -153,7 +148,7 @@
             r = c * 2 + q
             rel = []
             for k in range(slots):
-                raw = lax.rem(ids_ref[r, k] - me * own + own + total, total)
+                raw = lax.rem(ids_ref[k, r] - me * own + own + total, total)
                 rel.append(jnp.where(k < count_ref[r], raw, -1))
             row0 = pl.multiple_of(r * side, side)
             for s in range(side // sub):
@@ -182,6 +177,10 @@
     for copy in halos:
         copy.wait_recv()
 
+    def dpre_copy(c):
+        at = pl.ds(c * big, big)
+        return pltpu.make_async_copy(dpre_v.at[at], dpre_hbm.at[at], gout_sem.at[c])
+
     def middle(c, carry):
         at = pl.ds(pl.multiple_of(c * big, big), big)
         agg = part_v[at, :] + matmul(dense_v[at, :rows], wide_v[:rows, :])
@@ -191,6 +190,7 @@
         hidden_v[at, :] = (pre * gate).astype(BF16)
         d_pre = (dhid_v[at, :] * (gate * (1.0 + pre * (1.0 - gate)))).astype(BF16)
         dpre_v[at, :] = d_pre
+        dpre_copy(c).start()
         dagg_v[at, :] = matmul(d_pre, w_agg_t[...]).astype(BF16)
         return carry
 
@@ -213,14 +213,8 @@
         rims[way].start()
     own_v[...] = matmul(dense_t[rows : 2 * rows, :], dagg_v[...])
 
-    def ggrid_copy(c):
-        at = pl.ds(c * big, big)
-        return pltpu.make_async_copy(ggrid_v.at[at], ggrid_hbm.at[at], gout_sem.at[c])
-
     def late(c, carry):
         at = pl.ds(pl.multiple_of(c * big, big), big)
-        ggrid_v[at, :] = matmul(dpre_v[at, :], w_grid_t[...])
-        ggrid_copy(c).start()
         pred_v[:, at] = lax.dot_general(
             w_out_v[...], hidden_v[at, :], (((1,), (1,)), ((), ())), preferred_element_type=F32
         )
@@ -236,14 +230,76 @@
     for copy in rims:
         copy.wait_recv()
     d_sender = own_v[...] + (rx_v[0].astype(F32) + rx_v[1].astype(F32))
-    gmesh_v[...] = matmul((d_sender * slope).astype(BF16), w_send_t[...])
-    gmesh_copy = pltpu.make_async_copy(gmesh_v, gmesh_hbm, out_sem.at[1])
-    gmesh_copy.start()
+    dmesh_v[...] = (d_sender * slope).astype(BF16)
+    dmesh_copy = pltpu.make_async_copy(dmesh_v, dmesh_hbm, out_sem.at[1])
+    dmesh_copy.start()
 
     for copy in halos + rims:
         copy.wait_send()
     for c in range(bigs):
-        ggrid_copy(c).wait()
+        dpre_copy(c).wait()
+    pred_copy.wait()
+    dmesh_copy.wait()
+
+
+def finish(
+    pred_hbm,
+    dmesh_hbm,
+    dpre_hbm,
+    w_send_hbm,
+    w_grid_hbm,
+    pred_out,
+    gmesh_out,
+    ggrid_out,
+    pred_v,
+    dmesh_v,
+    dpre_v,
+    w_send_v,
+    w_grid_v,
+    w_grid_t,
+    gmesh_v,
+    ggrid_v,
+    in_sem,
+    dpre_sem,
+    out_sem,
+    gout_sem,
+):
+    last = (((1,), (1,)), ((), ()))
+    parts = dpre_sem.shape[0]
+    step = dpre_v.shape[0] // parts
+
+    w_grid_copy = pltpu.make_async_copy(w_grid_hbm, w_grid_v, in_sem.at[0])
+    dmesh_copy = pltpu.make_async_copy(dmesh_hbm, dmesh_v, in_sem.at[1])
+    w_send_copy = pltpu.make_async_copy(w_send_hbm, w_send_v, in_sem.at[2])
+    pred_read = pltpu.make_async_copy(pred_hbm, pred_v, in_sem.at[3])
+    pred_copy = pltpu.make_async_copy(pred_v, pred_out, out_sem.at[0])
+    gmesh_copy = pltpu.make_async_copy(gmesh_v, gmesh_out, out_sem.at[1])
+    reads, writes = [], []
+    for c in range(parts):
+        at = pl.ds(c * step, step)
+        reads.append(pltpu.make_async_copy(dpre_hbm.at[at], dpre_v.at[at], dpre_sem.at[c]))
+        writes.append(pltpu.make_async_copy(ggrid_v.at[at], ggrid_out.at[at], gout_sem.at[c]))
+    w_grid_copy.start()
+    for copy in reads:
+        copy.start()
+    dmesh_copy.start()
+    w_send_copy.start()
+    pred_read.start()
+    w_grid_copy.wait()
+    w_grid_t[...] = w_grid_v[...].T
+    for c in range(parts):
+        at = pl.ds(c * step, step)
+        reads[c].wait()
+        ggrid_v[at, :] = matmul(dpre_v[at, :], w_grid_t[...])
+        writes[c].start()
+    pred_read.wait()
+    pred_copy.start()
+    dmesh_copy.wait()
+    w_send_copy.wait()
+    gmesh_v[...] = lax.dot_general(dmesh_v[...], w_send_v[...], last, preferred_element_type=F32)
+    gmesh_copy.start()
+    for copy in writes:
+        copy.wait()
     pred_copy.wait()
     gmesh_copy.wait()
 
@@ -275,12 +331,12 @@
         return pltpu.VMEM(shape, dtype)
 
     square = (width, width)
-    return pl.pallas_call(
+    predictions, d_mesh_pre, d_pre = pl.pallas_call(
         functools.partial(kernel, lanes),
         out_shape=(
             jax.ShapeDtypeStruct((variables, grid_rows), F32),
-            jax.ShapeDtypeStruct((rows, width), F32),
-            jax.ShapeDtypeStruct((grid_rows, width), F32),
+            jax.ShapeDtypeStruct((rows, width), BF16),
+            jax.ShapeDtypeStruct((grid_rows, width), BF16),
         ),
         in_specs=[scalars] * 2 + [anywhere] * 8,
         out_specs=(anywhere,) * 3,
@@ -293,8 +349,6 @@
             vmem(*square),
             vmem(variables, width),
             vmem(variables, grid_rows),
-            vmem(*square),
-            vmem(*square),
             vmem(*square),
             vmem(rows, width, dtype=F32),
             vmem(wide, width),
@@ -310,8 +364,7 @@
             vmem(2, rows, width),
             vmem(2, rows, width),
             vmem(variables, grid_rows, dtype=F32),
-            vmem(rows, width, dtype=F32),
-            vmem(grid_rows, width, dtype=F32),
+            vmem(rows, width),
             pltpu.SemaphoreType.DMA((6,)),
             pltpu.SemaphoreType.DMA((chunks,)),
             pltpu.SemaphoreType.DMA((chunks,)),
@@ -329,7 +382,7 @@
             flops=7_000_000_000, bytes_accessed=11_000_000, transcendentals=1_000_000
         ),
     )(
-        sender_ids,
+        sender_ids.T,
         block_count,
         mesh_latent,
         grid_latent,
@@ -340,6 +393,31 @@
         w_out,
         cotangent,
     )
+    return pl.pallas_call(
+        finish,
+        out_shape=(
+            jax.ShapeDtypeStruct((variables, grid_rows), F32),
+            jax.ShapeDtypeStruct((rows, width), F32),
+            jax.ShapeDtypeStruct((grid_rows, width), F32),
+        ),
+        in_specs=[anywhere] * 5,
+        out_specs=(anywhere,) * 3,
+        scratch_shapes=[
+            vmem(variables, grid_rows, dtype=F32),
+            vmem(rows, width),
+            vmem(grid_rows, width),
+            vmem(*square),
+            vmem(*square),
+            vmem(*square),
+            vmem(rows, width, dtype=F32),
+            vmem(grid_rows, width, dtype=F32),
+            pltpu.SemaphoreType.DMA((4,)),
+            pltpu.SemaphoreType.DMA((chunks,)),
+            pltpu.SemaphoreType.DMA((2,)),
+            pltpu.SemaphoreType.DMA((chunks,)),
+        ],
+        compiler_params=pltpu.CompilerParams(vmem_limit_bytes=56 * 2**20),
+    )(predictions, d_mesh_pre, d_pre, w_send, w_grid)
 
 
 def solution(mesh):

time: 35.4 us -> 30.4 us (0.86)
  local copies, waits for them, and re-layouts: 8.97 us -> 0 us
  Pallas kernels: 25.4 us -> 29.6 us
    unnamed x4 -> x0, local copies, waits for them, and re-layouts: 8.97 us -> none
    pallas_call x0 -> x1, Pallas kernels: none -> 4.5 us  [per_device(): pl.pallas_call(finish, out_shape=(jax.ShapeDtypeStruct((variables, grid_r...]
where the time goes in v2:
time: 30.4 us; the launch traced here: 30.2 us
  Pallas kernels  29.6 us (97%)
  between operations  0.64 us (2%)
    pallas_call x1, Pallas kernels, per_device(): pl.pallas_call(functools.partial(kernel, lanes), out_shape=(jax.ShapeDtyp...  25.1 us
    pallas_call x1, Pallas kernels, per_device(): pl.pallas_call(finish, out_shape=(jax.ShapeDtypeStruct((variables, grid_r...  4.5 us

profile of v2, /device:TPU:0, one launch (start us, length us, event | category | flops | bytes accessed | tf_op | source)
XLA Modules:
  0.0 30.2 jit_solution(10219994498999957157)
XLA Ops:
  0.6 25.1 %shard_map.121 = (f32[83,1536]{1,0:T(8,128)}, bf16[256,512]{1,0:T(8,128)(2,1)}, bf16[1536,512]{1,0:T(8,128)(2,1)}) custom-call(s32[8,12]{1,0:T(8,128)} %bitcast.1, s32[12]{0:T(128)} %count_ref.1, bf16[256,512]{1,0:T(8,128)(2,1)} %mesh_hbm.1, bf16[1536,512]{1,0:T(8,128)(2,1)} %grid_hbm.1, bf16[12,8,128,128]{3,2,1,0:T(8,128)(2,1)} %tiles_hbm.1, ...), custom_call_target="tpu_custom_call" | custom-call | flops 7000000000 | bytes 11000000 | tf_op jit(solution)/shard_map/pallas_call | solution.py:334
  25.7 4.5 %shard_map.122 = (f32[83,1536]{1,0:T(8,128)}, f32[256,512]{1,0:T(8,128)}, f32[1536,512]{1,0:T(8,128)}) custom-call(f32[83,1536]{1,0:T(8,128)} %get-tuple-element.6.pred_hbm, bf16[256,512]{1,0:T(8,128)(2,1)} %get-tuple-element.7.dmesh_hbm, bf16[1536,512]{1,0:T(8,128)(2,1)} %get-tuple-element.8.dpre_hbm, bf16[512,512]{1,0:T(8,128)(2,1)} %w_send_hbm.3, ...), custom_call_target="tpu_custom_call" | custom-call | tf_op jit(solution)/shard_map/pallas_call | solution.py:396

commit v3 on v2

--- a/solution.py
+++ b/solution.py
@@ -70,7 +70,9 @@
     brecv_sem,
 ):
     me = lax.axis_index("lon")
-    right, left = lax.rem(me + 1, lanes), lax.rem(me + lanes - 1, lanes)
+    odd = lax.rem(me, 2)
+    far = lax.rem(me + lanes - 1 + 2 * odd, lanes)
+    near = lax.rem(me + lanes + 1 - 2 * odd, lanes)
     rows = mesh_v.shape[0]
     recv, slots, side, _ = tiles_v.shape
     grid_rows = grid_v.shape[0]
@@ -82,7 +84,7 @@
     bigs = grid_rows // big
 
     barrier = pltpu.get_barrier_semaphore()
-    for neighbour in (left, right):
+    for neighbour in (far, near):
         pl.semaphore_signal(barrier, inc=1, device_id={"lon": neighbour}, device_id_type=MESH)
 
     def load(at, src, dst):
@@ -119,11 +121,14 @@
 
     pl.semaphore_wait(barrier, 2)
 
+    rows_at = lambda start: pl.ds(pl.multiple_of(start, rows), rows)
+    far_at, near_at = rows_at(odd * 2 * rows), rows_at((1 - odd) * 2 * rows)
+
     def halo(way):
-        target, dst = (right, 0) if way == 0 else (left, 2 * rows)
+        target, dst = (far, near_at) if way == 0 else (near, far_at)
         return pltpu.make_async_remote_copy(
             src_ref=wide_v.at[pl.ds(rows, rows)],
-            dst_ref=wide_v.at[pl.ds(dst, rows)],
+            dst_ref=wide_v.at[dst],
             send_sem=fsend_sem.at[way],
             recv_sem=frecv_sem.at[way],
             device_id={"lon": target},
@@ -138,6 +143,7 @@
         c.wait()
     w_agg_t[...] = w_agg_v[...].T
 
+    halos[1].wait_recv()
     sub = 32
 
     def early(c, carry):
@@ -169,22 +175,22 @@
         dhid_v[at, :] = lax.dot_general(
             cot_v[:, at], w_out_v[...], (((0,), (0,)), ((), ())), preferred_element_type=F32
         )
-        part_v[at, :] = matmul(dense_v[at, rows : 2 * rows], wide_v[rows : 2 * rows, :])
+        part_v[at, :] = matmul(dense_v[at, rows : 2 * rows], wide_v[rows : 2 * rows, :]) + matmul(
+            dense_v[at, near_at], wide_v[near_at, :]
+        )
         return carry
 
     lax.fori_loop(0, chunks, early, 0)
 
-    for copy in halos:
-        copy.wait_recv()
+    halos[0].wait_recv()
 
     def dpre_copy(c):
         at = pl.ds(c * big, big)
         return pltpu.make_async_copy(dpre_v.at[at], dpre_hbm.at[at], gout_sem.at[c])
 
     def middle(c, carry):
-        at = pl.ds(pl.multiple_of(c * big, big), big)
-        agg = part_v[at, :] + matmul(dense_v[at, :rows], wide_v[:rows, :])
-        agg = agg + matmul(dense_v[at, 2 * rows :], wide_v[2 * rows :, :])
+        at = pl.ds(c * big, big)
+        agg = part_v[at, :] + matmul(dense_v[at, far_at], wide_v[far_at, :])
         pre = pre_v[at, :] + matmul(agg.astype(BF16), w_agg_v[...])
         gate = gate_of(pre)
         hidden_v[at, :] = (pre * gate).astype(BF16)
@@ -194,10 +200,11 @@
         dagg_v[at, :] = matmul(d_pre, w_agg_t[...]).astype(BF16)
         return carry
 
-    lax.fori_loop(0, bigs, middle, 0)
+    for c in range(bigs):
+        middle(c, 0)
 
     def rim(way):
-        target = left if way == 0 else right
+        target = far if way == 0 else near
         return pltpu.make_async_remote_copy(
             src_ref=tx_v.at[way],
             dst_ref=rx_v.at[way],
@@ -208,8 +215,8 @@
         )
 
     rims = [rim(0), rim(1)]
-    for way, start in ((0, 0), (1, 2 * rows)):
-        tx_v[way] = matmul(dense_t[start : start + rows, :], dagg_v[...]).astype(BF16)
+    for way, side_at in ((0, far_at), (1, near_at)):
+        tx_v[way] = matmul(dense_t[side_at, :], dagg_v[...]).astype(BF16)
         rims[way].start()
     own_v[...] = matmul(dense_t[rows : 2 * rows, :], dagg_v[...])
 

time: 30.4 us -> 29.2 us (0.961)
  Pallas kernels: 29.6 us -> 28.4 us
    pallas_call x1, Pallas kernels: 25.1 us -> 23.9 us  [per_device(): pl.pallas_call(functools.partial(kernel, lanes), out_shape=(jax.ShapeDtyp...]
where the time goes in v3:
time: 29.2 us; the launch traced here: 29 us
  Pallas kernels  28.4 us (97%)
  between operations  0.64 us (2%)
    pallas_call x1, Pallas kernels, per_device(): pl.pallas_call(functools.partial(kernel, lanes), out_shape=(jax.ShapeDtyp...  23.9 us
    pallas_call x1, Pallas kernels, per_device(): pl.pallas_call(finish, out_shape=(jax.ShapeDtypeStruct((variables, grid_r...  4.5 us

profile of v3, /device:TPU:0, one launch (start us, length us, event | category | flops | bytes accessed | tf_op | source)
XLA Modules:
  0.0 29.0 jit_solution(11640896155900353460)
XLA Ops:
  0.6 23.9 %shard_map.121 = (f32[83,1536]{1,0:T(8,128)}, bf16[256,512]{1,0:T(8,128)(2,1)}, bf16[1536,512]{1,0:T(8,128)(2,1)}) custom-call(s32[8,12]{1,0:T(8,128)} %bitcast.1, s32[12]{0:T(128)} %count_ref.1, bf16[256,512]{1,0:T(8,128)(2,1)} %mesh_hbm.1, bf16[1536,512]{1,0:T(8,128)(2,1)} %grid_hbm.1, bf16[12,8,128,128]{3,2,1,0:T(8,128)(2,1)} %tiles_hbm.1, ...), custom_call_target="tpu_custom_call" | custom-call | flops 7000000000 | bytes 11000000 | tf_op jit(solution)/shard_map/pallas_call | solution.py:341
  24.5 4.5 %shard_map.122 = (f32[83,1536]{1,0:T(8,128)}, f32[256,512]{1,0:T(8,128)}, f32[1536,512]{1,0:T(8,128)}) custom-call(f32[83,1536]{1,0:T(8,128)} %get-tuple-element.6.pred_hbm, bf16[256,512]{1,0:T(8,128)(2,1)} %get-tuple-element.7.dmesh_hbm, bf16[1536,512]{1,0:T(8,128)(2,1)} %get-tuple-element.8.dpre_hbm, bf16[512,512]{1,0:T(8,128)(2,1)} %w_send_hbm.3, ...), custom_call_target="tpu_custom_call" | custom-call | tf_op jit(solution)/shard_map/pallas_call | solution.py:403
